TPU v7x, 128 devices: a whole 4x4x4 slice. The times are simulated.
128 devices in a mesh: gy: 8 (over z, y_lo), gx: 16 (over x, y_hi, core).
Axes of the slice: x: 4, y: 4 (y_hi: 2, y_lo: 2; y = y_hi * 2 + y_lo), z: 4, core: 2. Of those that a mesh axis runs over, the one named last changes fastest.
Arguments:
- radar_input: bfloat16 [512, 1024, 256], P('gy', 'gx'), may hold values from -6 to 6
- conv_weight: bfloat16 [3, 3, 256, 256], replicated, may hold values from -0.125 to 0.125
- conv_bias: float32 [256], replicated, may hold values from -3 to 3
- row_gain: float32 [256], replicated, may hold values from 0.1 to 1.9
- row_qkv: bfloat16 [256, 768], replicated, may hold values from -8 to 8
- row_out: bfloat16 [256, 256], replicated, may hold values from -0.375 to 0.375
- col_gain: float32 [256], replicated, may hold values from 0.1 to 1.9
- col_qkv: bfloat16 [256, 768], replicated, may hold values from -8 to 8
- col_out: bfloat16 [256, 256], replicated, may hold values from -0.375 to 0.375
Outputs:
- block_output: bfloat16 [512, 1024, 256], P('gy', 'gx')
All inputs are finite; a program needn't handle non-finite values.
Results may differ from a plain program's by a relative error of at most 0.012.
Values may be sent and summed in bfloat16 or wider, within the bound.
No kernel may reach another device: no remote copies, remote signals or barrier semaphores. Data moves between devices by JAX's collectives and lax.ppermute only.
A program may use at most 128 MiB of HBM per device.

v0:
```python
import jax
import jax.numpy as jnp
from jax import lax
from jax.sharding import PartitionSpec as P

HEADS = 8


def with_halo(shard, sides, width):
    for axis, dim in sides:
        devices, length = (lax.axis_size(axis), shard.shape[dim])
        up = [(i, (i + 1) % devices) for i in range(devices - 1)]
        down = [(j, i) for i, j in up]
        last = lax.slice_in_dim(shard, length - width, length, axis=dim)
        initial = lax.slice_in_dim(shard, 0, width, axis=dim)
        before = lax.ppermute(last, axis, up)
        after = lax.ppermute(initial, axis, down)
        shard = jnp.concatenate([before, shard, after], axis=dim)
    return shard


def layer_norm(grid, gain):
    values = grid.astype(jnp.float32)
    center = jnp.mean(values, axis=-1, keepdims=True)
    spread = jnp.mean((values - center) ** 2, axis=-1, keepdims=True)
    return ((values - center) * lax.rsqrt(spread + 1e-05) * gain).astype(jnp.bfloat16)


def convolve(padded, source, conv_weight, conv_bias):
    rows, cols, chans = source.shape
    total = jnp.zeros((rows * cols, conv_weight.shape[3]), jnp.float32)
    for dy in range(3):
        for dx in range(3):
            window = padded[dy : dy + rows, dx : dx + cols].reshape(rows * cols, chans)
            total = total + jnp.dot(window, conv_weight[dy, dx], preferred_element_type=jnp.float32)
    pre = total.reshape(rows, cols, -1) + conv_bias
    return (source.astype(jnp.float32) + jax.nn.gelu(pre)).astype(jnp.bfloat16)


def sequence_attention(queries, keys, values):
    length, chans = queries.shape
    heads = HEADS
    width = chans // heads
    qh = queries.reshape(length, heads, width)
    kh = keys.reshape(length, heads, width)
    vh = values.reshape(length, heads, width)
    block = min(length, 512)
    pieces = []
    for start in range(0, length, block):
        scores = jnp.einsum(
            "qhd,khd->hqk", qh[start : start + block], kh, preferred_element_type=jnp.float32
        ) * width ** (-0.5)
        top = jnp.max(scores, axis=-1, keepdims=True)
        expo = jnp.exp(scores - top)
        weights = (expo / jnp.sum(expo, axis=-1, keepdims=True)).astype(jnp.bfloat16)
        mixed = jnp.einsum("hqk,khd->qhd", weights, vh, preferred_element_type=jnp.float32)
        pieces.append(mixed.astype(jnp.bfloat16).reshape(-1, chans))
    return jnp.concatenate(pieces, axis=0)


def attend_all(queries, keys, values, axis):
    count = queries.shape[axis]

    def step(index, result):
        one_q = lax.dynamic_index_in_dim(queries, index, axis, keepdims=False)
        one_k = lax.dynamic_index_in_dim(keys, index, axis, keepdims=False)
        one_v = lax.dynamic_index_in_dim(values, index, axis, keepdims=False)
        mixed = sequence_attention(one_q, one_k, one_v)
        return lax.dynamic_update_index_in_dim(result, mixed, index, axis)

    return lax.fori_loop(0, count, step, jnp.zeros(queries.shape, jnp.bfloat16))


def project(grid, gain, qkv_weight):
    chans = grid.shape[-1]
    normed = layer_norm(grid, gain)
    joined = jnp.dot(
        normed.reshape(-1, chans), qkv_weight, preferred_element_type=jnp.float32
    ).astype(jnp.bfloat16)
    joined = joined.reshape(grid.shape[:-1] + (3 * chans,))
    return (joined[..., :chans], joined[..., chans : 2 * chans], joined[..., 2 * chans :])


def finish(grid, mixed, out_weight):
    chans = grid.shape[-1]
    update = jnp.dot(
        mixed.reshape(-1, chans), out_weight, preferred_element_type=jnp.float32
    ).reshape(grid.shape)
    return (grid.astype(jnp.float32) + update).astype(jnp.bfloat16)


def shards(
    radar_input, conv_weight, conv_bias, row_gain, row_qkv, row_out, col_gain, col_qkv, col_out
):
    padded = with_halo(radar_input, (("gy", 0), ("gx", 1)), 1)
    hidden = convolve(padded, radar_input, conv_weight, conv_bias)
    queries, keys, values = project(hidden, row_gain, row_qkv)
    queries, keys, values = (
        lax.all_to_all(queries, "gx", split_axis=0, concat_axis=1, tiled=True),
        lax.all_to_all(keys, "gx", split_axis=0, concat_axis=1, tiled=True),
        lax.all_to_all(values, "gx", split_axis=0, concat_axis=1, tiled=True),
    )
    mixed = attend_all(queries, keys, values, 0)
    mixed = lax.all_to_all(mixed, "gx", split_axis=1, concat_axis=0, tiled=True)
    second = finish(hidden, mixed, row_out)
    queries, keys, values = project(second, col_gain, col_qkv)
    queries, keys, values = (
        lax.all_to_all(queries, "gy", split_axis=1, concat_axis=0, tiled=True),
        lax.all_to_all(keys, "gy", split_axis=1, concat_axis=0, tiled=True),
        lax.all_to_all(values, "gy", split_axis=1, concat_axis=0, tiled=True),
    )
    mixed = attend_all(queries, keys, values, 1)
    mixed = lax.all_to_all(mixed, "gy", split_axis=0, concat_axis=1, tiled=True)
    return finish(second, mixed, col_out)


def solution(mesh):
    in_specs = (P("gy", "gx", None), P(), P(), P(), P(), P(), P(), P(), P())
    out_specs = P("gy", "gx", None)
    return jax.shard_map(shards, mesh=mesh, in_specs=in_specs, out_specs=out_specs, check_vma=False)
```

profile of v0, /device:TPU:0, one launch (start us, length us, event | category | flops | bytes accessed | tf_op | source)
XLA Modules:
  0.0 587.2 jit_solution(1748125187543663870)
XLA Ops:
  6.0 4.2 collective-permute-done.1
  21.5 7.7 %pad_maximum_fusion.2 = (bf16[64,64,256]{2,1,0:T(8,128)(2,1)S(1)}, bf16[64,64,256]{2,1,0:T(8,128)(2,1)S(1)}, bf16[64,64,256]{2,1,0:T(8,128)(2,1)S(1)}, bf16[64,6...) fusion(bf16[66,64,256]{2,1,0:T(8,128)(2,1)S(1)} %constant_dynamic-update-slice_fusion., ...), kind=kLoop, calls=%fused_computation.92 | loop fusion | flops 25165824 | bytes 14813184 | tf_op jit(solution)/shard_map/concatenate | solution.py:18
  45.0 39.1 %all_to_all.138 = bf16[64,64,256]{2,1,0:T(8,128)(2,1)} all-to-all(bf16[64,64,256]{2,1,0:T(8,128)(2,1)S(1)} %get-tuple-element.264), channel_id=1, replica_groups=mesh['gy'=8,'gx'=16] {'gx'}, dimensions={0} | all-to-all | bytes 4194304 | tf_op jit(solution)/shard_map/all_to_all | solution.py:101
  84.1 32.5 %all_to_all.139 = bf16[64,64,256]{2,1,0:T(8,128)(2,1)} all-to-all(bf16[64,64,256]{2,1,0:T(8,128)(2,1)S(1)} %get-tuple-element.263), channel_id=1, replica_groups=mesh['gy'=8,'gx'=16] {'gx'}, dimensions={0} | all-to-all | bytes 4194304 | tf_op jit(solution)/shard_map/all_to_all | solution.py:99
  125.2 24.4 %all-to-all-done.2 = bf16[64,64,256]{2,1,0:T(8,128)(2,1)S(1)} async-done(((bf16[64,64,256]{2,1,0:T(8,128)(2,1)}), bf16[64,64,256]{2,1,0:T(8,128)(2,1)S(1)}, u32[]{:S(2)}, u32[]{:S(2)}) %all-to-all-start.2) | async-done | bytes 2097184 | tf_op jit(solution)/shard_map/all_to_all | solution.py:100
  151.0 151.2 %while.26 = (s32[]{:T(128)}, bf16[4,1024,256]{1,2,0:T(8,128)(2,1)}, bf16[4,1024,256]{2,1,0:T(8,128)(2,1)}, bf16[4,1024,256]{2,1,0:T(8,128)(2,1)}, bf16[4,1024,25...) while((s32[]{:T(128)}, bf16[4,1024,256]{1,2,0:T(8,128)(2,1)}, bf16[4,1024,256]{2,1,0:T(8,128)(2,1)}, ...), condition=%wide.region_7.8_spmd, body=%wide.region_2.7_spmd.sunk | while | flops 1116997632 | bytes 77660280 | solution.py:71
  154.0 8.5 %fusion.142 = (f32[8,512]{1,0:T(8,128)S(1)}, f32[8,512,1024]{2,1,0:T(8,128)}) fusion(bf16[512,8,32]{0,2,1:T(8,128)(2,1)S(1)} %bitcast.202, bf16[1024,8,32]{0,2,1:T(8,128)(2,1)S(1)} %bitcast.181), kind=kOutput, calls=%fused_computation.126.clone.1 | convolution fusion | flops 281019392 | bytes 17580032 | tf_op jit(solution)/shard_map/while/body/eval_jaxpr/sub | solution.py:54
  162.4 8.4 %fusion.143 = bf16[8,32,512]{2,1,0:T(8,128)(2,1)S(1)} fusion(bf16[1024,8,32]{0,2,1:T(8,128)(2,1)S(1)} %bitcast.179, f32[8,512,1024]{2,1,0:T(8,128)} %get-tuple-element.355, f32[8,512]{1,0:T(8,128)S(1)} %get-tuple-element.356), kind=kOutput, calls=%fused_computation.16.clone.1 | convolution fusion | flops 276955136 | bytes 17580032 | tf_op jit(solution)/shard_map/while/body/eval_jaxpr/hqk,khd->qhd/dot_general | solution.py:56
  171.0 8.5 %fusion.144 = (f32[8,512]{1,0:T(8,128)S(1)}, f32[8,512,1024]{2,1,0:T(8,128)}) fusion(bf16[512,8,32]{0,2,1:T(8,128)(2,1)S(1)} %bitcast.203, bf16[1024,8,32]{0,2,1:T(8,128)(2,1)S(1)} %bitcast.182), kind=kOutput, calls=%fused_computation.127.clone.1 | convolution fusion | flops 281019392 | bytes 17580032 | tf_op jit(solution)/shard_map/while/body/eval_jaxpr/sub | solution.py:54
  179.5 8.4 %fusion.145 = bf16[8,32,512]{2,1,0:T(8,128)(2,1)S(1)} fusion(bf16[1024,8,32]{0,2,1:T(8,128)(2,1)S(1)} %bitcast.180, f32[8,512,1024]{2,1,0:T(8,128)} %get-tuple-element.358, f32[8,512]{1,0:T(8,128)S(1)} %get-tuple-element.359), kind=kOutput, calls=%fused_computation.17.clone.1 | convolution fusion | flops 276955136 | bytes 17580032 | tf_op jit(solution)/shard_map/while/body/eval_jaxpr/hqk,khd->qhd/dot_general | solution.py:56
  191.8 8.5 %fusion.142 = (f32[8,512]{1,0:T(8,128)S(1)}, f32[8,512,1024]{2,1,0:T(8,128)}) fusion(bf16[512,8,32]{0,2,1:T(8,128)(2,1)S(1)} %bitcast.202, bf16[1024,8,32]{0,2,1:T(8,128)(2,1)S(1)} %bitcast.181), kind=kOutput, calls=%fused_computation.126.clone.1 | convolution fusion | flops 281019392 | bytes 17580032 | tf_op jit(solution)/shard_map/while/body/eval_jaxpr/sub | solution.py:54
  200.2 8.4 %fusion.143 = bf16[8,32,512]{2,1,0:T(8,128)(2,1)S(1)} fusion(bf16[1024,8,32]{0,2,1:T(8,128)(2,1)S(1)} %bitcast.179, f32[8,512,1024]{2,1,0:T(8,128)} %get-tuple-element.355, f32[8,512]{1,0:T(8,128)S(1)} %get-tuple-element.356), kind=kOutput, calls=%fused_computation.16.clone.1 | convolution fusion | flops 276955136 | bytes 17580032 | tf_op jit(solution)/shard_map/while/body/eval_jaxpr/hqk,khd->qhd/dot_general | solution.py:56
  208.8 8.5 %fusion.144 = (f32[8,512]{1,0:T(8,128)S(1)}, f32[8,512,1024]{2,1,0:T(8,128)}) fusion(bf16[512,8,32]{0,2,1:T(8,128)(2,1)S(1)} %bitcast.203, bf16[1024,8,32]{0,2,1:T(8,128)(2,1)S(1)} %bitcast.182), kind=kOutput, calls=%fused_computation.127.clone.1 | convolution fusion | flops 281019392 | bytes 17580032 | tf_op jit(solution)/shard_map/while/body/eval_jaxpr/sub | solution.py:54
  217.3 8.4 %fusion.145 = bf16[8,32,512]{2,1,0:T(8,128)(2,1)S(1)} fusion(bf16[1024,8,32]{0,2,1:T(8,128)(2,1)S(1)} %bitcast.180, f32[8,512,1024]{2,1,0:T(8,128)} %get-tuple-element.358, f32[8,512]{1,0:T(8,128)S(1)} %get-tuple-element.359), kind=kOutput, calls=%fused_computation.17.clone.1 | convolution fusion | flops 276955136 | bytes 17580032 | tf_op jit(solution)/shard_map/while/body/eval_jaxpr/hqk,khd->qhd/dot_general | solution.py:56
  229.6 8.5 %fusion.142 = (f32[8,512]{1,0:T(8,128)S(1)}, f32[8,512,1024]{2,1,0:T(8,128)}) fusion(bf16[512,8,32]{0,2,1:T(8,128)(2,1)S(1)} %bitcast.202, bf16[1024,8,32]{0,2,1:T(8,128)(2,1)S(1)} %bitcast.181), kind=kOutput, calls=%fused_computation.126.clone.1 | convolution fusion | flops 281019392 | bytes 17580032 | tf_op jit(solution)/shard_map/while/body/eval_jaxpr/sub | solution.py:54
  238.0 8.4 %fusion.143 = bf16[8,32,512]{2,1,0:T(8,128)(2,1)S(1)} fusion(bf16[1024,8,32]{0,2,1:T(8,128)(2,1)S(1)} %bitcast.179, f32[8,512,1024]{2,1,0:T(8,128)} %get-tuple-element.355, f32[8,512]{1,0:T(8,128)S(1)} %get-tuple-element.356), kind=kOutput, calls=%fused_computation.16.clone.1 | convolution fusion | flops 276955136 | bytes 17580032 | tf_op jit(solution)/shard_map/while/body/eval_jaxpr/hqk,khd->qhd/dot_general | solution.py:56
  246.6 8.5 %fusion.144 = (f32[8,512]{1,0:T(8,128)S(1)}, f32[8,512,1024]{2,1,0:T(8,128)}) fusion(bf16[512,8,32]{0,2,1:T(8,128)(2,1)S(1)} %bitcast.203, bf16[1024,8,32]{0,2,1:T(8,128)(2,1)S(1)} %bitcast.182), kind=kOutput, calls=%fused_computation.127.clone.1 | convolution fusion | flops 281019392 | bytes 17580032 | tf_op jit(solution)/shard_map/while/body/eval_jaxpr/sub | solution.py:54
  255.1 8.4 %fusion.145 = bf16[8,32,512]{2,1,0:T(8,128)(2,1)S(1)} fusion(bf16[1024,8,32]{0,2,1:T(8,128)(2,1)S(1)} %bitcast.180, f32[8,512,1024]{2,1,0:T(8,128)} %get-tuple-element.358, f32[8,512]{1,0:T(8,128)S(1)} %get-tuple-element.359), kind=kOutput, calls=%fused_computation.17.clone.1 | convolution fusion | flops 276955136 | bytes 17580032 | tf_op jit(solution)/shard_map/while/body/eval_jaxpr/hqk,khd->qhd/dot_general | solution.py:56
  267.4 8.5 %fusion.142 = (f32[8,512]{1,0:T(8,128)S(1)}, f32[8,512,1024]{2,1,0:T(8,128)}) fusion(bf16[512,8,32]{0,2,1:T(8,128)(2,1)S(1)} %bitcast.202, bf16[1024,8,32]{0,2,1:T(8,128)(2,1)S(1)} %bitcast.181), kind=kOutput, calls=%fused_computation.126.clone.1 | convolution fusion | flops 281019392 | bytes 17580032 | tf_op jit(solution)/shard_map/while/body/eval_jaxpr/sub | solution.py:54
  275.8 8.4 %fusion.143 = bf16[8,32,512]{2,1,0:T(8,128)(2,1)S(1)} fusion(bf16[1024,8,32]{0,2,1:T(8,128)(2,1)S(1)} %bitcast.179, f32[8,512,1024]{2,1,0:T(8,128)} %get-tuple-element.355, f32[8,512]{1,0:T(8,128)S(1)} %get-tuple-element.356), kind=kOutput, calls=%fused_computation.16.clone.1 | convolution fusion | flops 276955136 | bytes 17580032 | tf_op jit(solution)/shard_map/while/body/eval_jaxpr/hqk,khd->qhd/dot_general | solution.py:56
  284.4 8.5 %fusion.144 = (f32[8,512]{1,0:T(8,128)S(1)}, f32[8,512,1024]{2,1,0:T(8,128)}) fusion(bf16[512,8,32]{0,2,1:T(8,128)(2,1)S(1)} %bitcast.203, bf16[1024,8,32]{0,2,1:T(8,128)(2,1)S(1)} %bitcast.182), kind=kOutput, calls=%fused_computation.127.clone.1 | convolution fusion | flops 281019392 | bytes 17580032 | tf_op jit(solution)/shard_map/while/body/eval_jaxpr/sub | solution.py:54
  292.9 8.4 %fusion.145 = bf16[8,32,512]{2,1,0:T(8,128)(2,1)S(1)} fusion(bf16[1024,8,32]{0,2,1:T(8,128)(2,1)S(1)} %bitcast.180, f32[8,512,1024]{2,1,0:T(8,128)} %get-tuple-element.358, f32[8,512]{1,0:T(8,128)S(1)} %get-tuple-element.359), kind=kOutput, calls=%fused_computation.17.clone.1 | convolution fusion | flops 276955136 | bytes 17580032 | tf_op jit(solution)/shard_map/while/body/eval_jaxpr/hqk,khd->qhd/dot_general | solution.py:56
  305.3 33.9 %all_to_all.140 = bf16[4,1024,256]{2,0,1:T(4,128)(2,1)S(1)} all-to-all(bf16[4,1024,256]{2,0,1:T(4,128)(2,1)S(1)} %copy.54), channel_id=1, replica_groups=mesh['gy'=8,'gx'=16] {'gx'}, dimensions={1} | all-to-all | bytes 4194304 | tf_op jit(solution)/shard_map/all_to_all | solution.py:104
  352.0 7.0 %all-to-all-start.4 = ((bf16[64,64,256]{2,0,1:T(8,128)(2,1)}), bf16[64,64,256]{2,0,1:T(8,128)(2,1)}, u32[]{:S(2)}, u32[]{:S(2)}) async-start(bf16[64,64,256]{2,0,1:T(8,128)(2,1)} %copy.78), calls=%async_computation.4 | async-start | bytes 4194304 | tf_op jit(solution)/shard_map/all_to_all | solution.py:110
  363.1 22.3 %all-to-all-done.4 = bf16[64,64,256]{2,0,1:T(8,128)(2,1)} async-done(((bf16[64,64,256]{2,0,1:T(8,128)(2,1)}), bf16[64,64,256]{2,0,1:T(8,128)(2,1)}, u32[]{:S(2)}, u32[]{:S(2)}) %all-to-all-start.4) | async-done | bytes 2097184 | tf_op jit(solution)/shard_map/all_to_all | solution.py:110
  385.4 4.3 all-to-all-start.5
  393.9 21.5 %all-to-all-done.5 = bf16[64,64,256]{2,0,1:T(8,128)(2,1)} async-done(((bf16[64,64,256]{2,0,1:T(8,128)(2,1)}), bf16[64,64,256]{2,0,1:T(8,128)(2,1)}, u32[]{:S(2)}, u32[]{:S(2)}) %all-to-all-start.5) | async-done | bytes 2097184 | tf_op jit(solution)/shard_map/all_to_all | solution.py:108
  415.3 4.6 all-to-all-start.6
  424.1 4.3 copy.66
  432.6 4.3 copy.67
  437.0 8.6 %all-to-all-done.6 = bf16[64,64,256]{2,0,1:T(8,128)(2,1)} async-done(((bf16[64,64,256]{2,0,1:T(8,128)(2,1)}), bf16[64,64,256]{2,0,1:T(8,128)(2,1)}, u32[]{:S(2)}, u32[]{:S(2)}) %all-to-all-start.6) | async-done | bytes 2097184 | tf_op jit(solution)/shard_map/all_to_all | solution.py:109
  449.7 4.4 copy.68
  454.1 96.2 %while.27 = (s32[]{:T(128)}, bf16[512,8,256]{0,2,1:T(8,128)(2,1)}, bf16[512,8,256]{0,2,1:T(8,128)(2,1)}, bf16[512,8,256]{0,2,1:T(8,128)(2,1)}, bf16[512,8,256]{0,2,1:T(8,128)(2,1)}, /*index=5*/s32[]{:T(128)}) while((s32[]{:T(128)}, bf16[512,8,256]{0,2,1:T(8,128)(2,1)}, bf16[512,8,256]{0,2,1:T(8,128)(2,1)}, bf16[512,8,256]{0,2,1:T(8,128)(2,1)}, ...), condition=%wide.region_13.14_spmd, body=%wide.region_10.13_spmd.sunk | while | flops 279052800 | bytes 19955800 | solution.py:71
  456.1 5.0 fusion.150
  461.2 4.2 fusion.151
  468.1 5.0 fusion.150
  473.2 4.2 fusion.151
  480.2 5.0 fusion.150
  492.2 5.0 fusion.150
  504.2 5.0 fusion.150
  509.3 4.2 fusion.151
  516.2 5.0 fusion.150
  521.3 4.2 fusion.151
  528.3 5.0 fusion.150
  533.3 4.2 fusion.151
  540.3 5.0 fusion.150
  550.3 4.5 copy.69
  554.8 30.0 %all_to_all.141 = bf16[512,8,256]{2,1,0:T(8,128)(2,1)S(1)} all-to-all(bf16[512,8,256]{2,1,0:T(8,128)(2,1)} %copy.69), channel_id=1, replica_groups=mesh['gy'=8,'gx'=16] {'gy'}, dimensions={0} | all-to-all | bytes 4194304 | tf_op jit(solution)/shard_map/all_to_all | solution.py:113
  (132 shorter events, 131.9 us)
Async XLA Ops:
  0.0 40.9 %copy-start = (bf16[256,768]{1,0:T(8,128)(2,1)S(1)}, bf16[256,768]{1,0:T(8,128)(2,1)}, u32[]{:S(2)}) copy-start(bf16[256,768]{1,0:T(8,128)(2,1)} %param.17) | copy-start | bytes 1179652
  0.8 5.1 collective-permute-start
  4.4 5.8 collective-permute-start.1
  6.0 10.5 %copy-start.6 = (bf16[3,3,256,256]{3,2,1,0:T(8,128)(2,1)S(1)}, bf16[3,3,256,256]{3,2,1,0:T(8,128)(2,1)}, u32[]{:S(2)}) copy-start(bf16[3,3,256,256]{3,2,1,0:T(8,128)(2,1)} %param.14) | copy-start | bytes 3538948
  13.9 4.0 collective-permute-start.2
  15.2 6.4 %collective-permute-start.3 = (bf16[66,1,256]{2,1,0:T(2,128)(2,1)S(1)}, bf16[66,1,256]{2,1,0:T(2,128)(2,1)S(1)}, u32[]{:S(2)}, u32[]{:S(2)}) collective-permute-start(bf16[66,1,256]{2,1,0:T(2,128)(2,1)S(1)} %get-tuple-element.275), channel_id=1, source_target_pairs={{1,0},{2,1},{3,2},{4,3},{5,4},{6,5},{7,6},{8,7},{9,8},{10,9},{11,1... | collective-permute-start | bytes 101384 | tf_op jit(solution)/shard_map/ppermute | solution.py:17
  31.4 1.6 copy-start.4
  34.5 1.2 copy-start.10
  38.0 2.9 copy-start.2
  38.1 1.4 copy-start.11
  116.6 32.9 %all-to-all-start.2 = ((bf16[64,64,256]{2,1,0:T(8,128)(2,1)}), bf16[64,64,256]{2,1,0:T(8,128)(2,1)S(1)}, u32[]{:S(2)}, u32[]{:S(2)}) async-start(bf16[64,64,256]{2,1,0:T(8,128)(2,1)} %get-tuple-element.262), calls=%async_computation.2 | async-start | bytes 4194304 | tf_op jit(solution)/shard_map/all_to_all | solution.py:100
  120.4 3.3 copy-start.5
  339.5 1.6 copy-start.3
  339.5 1.6 copy-start.8
  341.9 1.4 copy-start.12
  343.2 1.5 copy-start.7
  352.0 33.4 %all-to-all-start.4 = ((bf16[64,64,256]{2,0,1:T(8,128)(2,1)}), bf16[64,64,256]{2,0,1:T(8,128)(2,1)}, u32[]{:S(2)}, u32[]{:S(2)}) async-start(bf16[64,64,256]{2,0,1:T(8,128)(2,1)} %copy.78), calls=%async_computation.4 | async-start | bytes 4194304 | tf_op jit(solution)/shard_map/all_to_all | solution.py:110
  385.4 29.9 %all-to-all-start.5 = ((bf16[64,64,256]{2,0,1:T(8,128)(2,1)}), bf16[64,64,256]{2,0,1:T(8,128)(2,1)}, u32[]{:S(2)}, u32[]{:S(2)}) async-start(bf16[64,64,256]{2,0,1:T(8,128)(2,1)} %copy.79), calls=%async_computation.5 | async-start | bytes 4194304 | tf_op jit(solution)/shard_map/all_to_all | solution.py:108
  415.3 30.2 %all-to-all-start.6 = ((bf16[64,64,256]{2,0,1:T(8,128)(2,1)}), bf16[64,64,256]{2,0,1:T(8,128)(2,1)}, u32[]{:S(2)}, u32[]{:S(2)}) async-start(bf16[64,64,256]{2,0,1:T(8,128)(2,1)} %copy.80), calls=%async_computation.6 | async-start | bytes 4194304 | tf_op jit(solution)/shard_map/all_to_all | solution.py:109
  554.8 30.0 %copy-start.9 = (bf16[256,256]{1,0:T(8,128)(2,1)S(1)}, bf16[256,256]{1,0:T(8,128)(2,1)}, u32[]{:S(2)}) copy-start(bf16[256,256]{1,0:T(8,128)(2,1)} %param.21) | copy-start | bytes 393220
  584.8 2.0 copy-start.1
where the time goes:
time: 598 us; the launch traced here: 587 us
  matrix products  223 us (37%)
  blocking collectives  136 us (23%)
  local copies, waits for them, and re-layouts  93.3 us (16%)
  waiting for transfers between devices  84.9 us (14%)
  starting transfers between devices  27.1 us (5%)
  other arithmetic  22.6 us (4%)
    sub x16, matrix products, sequence_attention(): expo = jnp.exp(scores - top)  108 us
    dot_general x16, matrix products, sequence_attention(): jnp.einsum('hqk,khd->qhd', weights, vh, preferred_element_type=jnp.float32)  101 us
    all_to_all x1, blocking collectives, shards(): lax.all_to_all(values, 'gx', split_axis=0, concat_axis=1, tiled=True)  39.1 us
    all_to_all x1, blocking collectives, shards(): mixed = lax.all_to_all(mixed, 'gx', split_axis=1, concat_axis=0, tiled=True)  33.9 us
    all_to_all x1, blocking collectives, shards(): lax.all_to_all(queries, 'gx', split_axis=0, concat_axis=1, tiled=True)  32.5 us
    all_to_all x1, blocking collectives, shards(): mixed = lax.all_to_all(mixed, 'gy', split_axis=0, concat_axis=1, tiled=True)  30 us
    all_to_all x1, waiting for transfers between devices, shards(): lax.all_to_all(keys, 'gx', split_axis=0, concat_axis=1, tiled=True)  24.4 us
    all_to_all x1, waiting for transfers between devices, shards(): lax.all_to_all(values, 'gy', split_axis=1, concat_axis=0, tiled=True)  22.3 us
  transfers between devices with their start and end apart: 8, of which 7 were waited for; matrix products, arithmetic and copies ran while one was open for 5% of the time, Pallas kernels for 0%

commit v1 on v0

v1 whole, which is shorter than its diff:
```python
import functools

import jax
import jax.numpy as jnp
from jax import lax
from jax.experimental import pallas as pl
from jax.experimental.pallas import tpu as pltpu
from jax.sharding import PartitionSpec as P

HEADS = 8
WIDTH = 32
C = 256
SCORE_SCALE = 1.4426950408889634 / 32**0.5
SAFE_SQUARE = 62.0**2
VMEM_LIMIT = 56 * 2**20
F32 = jnp.float32
BF16 = jnp.bfloat16


def dot(a, b):
    return jnp.dot(a, b, preferred_element_type=F32)


def dot_nt(a, b):
    return lax.dot_general(a, b, (((1,), (1,)), ((), ())), preferred_element_type=F32)


def dot_tn(a, b):
    return lax.dot_general(a, b, (((0,), (0,)), ((), ())), preferred_element_type=F32)


def normalize(values, gain):
    center = jnp.mean(values, axis=-1, keepdims=True)
    shifted = values - center
    spread = jnp.mean(shifted * shifted, axis=-1, keepdims=True)
    return (shifted * lax.rsqrt(spread + 1e-05) * gain).astype(BF16)


def projections(normed, wq_t, wk, wv_t, k_ref, qt_ref, vt_ref):
    keys = dot(normed, wk)
    k_ref[...] = keys.astype(BF16)
    queries = dot_nt(wq_t, normed) * SCORE_SCALE
    qt_ref[...] = queries.astype(BF16)
    vt_ref[...] = dot_nt(wv_t, normed).astype(BF16)
    length = normed.shape[0]
    q_norms = jnp.sum((queries * queries).reshape(HEADS, WIDTH, length), axis=1)
    head_of = lax.broadcasted_iota(jnp.int32, (C, 128), 0) // WIDTH
    column = lax.broadcasted_iota(jnp.int32, (C, 128), 1)
    pick = jnp.where(head_of == column, 1.0, 0.0).astype(BF16)
    k_norms = dot((keys * keys).astype(BF16), pick)
    return jnp.max(q_norms) * jnp.max(k_norms) <= SAFE_SQUARE


def attend(safe, k_ref, qt_ref, vt_ref, att_ref, length, tile):
    ones = jnp.ones((16, length), BF16)

    def head_rows(head):
        return slice(head * WIDTH, (head + 1) * WIDTH)

    def finish(mixed):
        return (mixed[:WIDTH] / mixed[WIDTH : WIDTH + 1]).astype(BF16)

    @pl.when(safe)
    def _():
        def step(t, carry):
            cols = pl.ds(pl.multiple_of(t * tile, tile), tile)
            for head in range(HEADS):
                rows = head_rows(head)
                values = jnp.concatenate([vt_ref[rows, :], ones], axis=0)
                scores = dot(k_ref[:, rows], qt_ref[rows, cols])
                expo = jnp.exp2(scores).astype(BF16)
                att_ref[rows, cols] = finish(dot(values, expo))
            return carry

        lax.fori_loop(0, length // tile, step, 0)

    @pl.when(jnp.logical_not(safe))
    def _():
        def step(t, carry):
            cols = pl.ds(pl.multiple_of(t * 256, 256), 256)
            for head in range(HEADS):
                rows = head_rows(head)
                values = jnp.concatenate([vt_ref[rows, :], ones], axis=0)
                scores = dot(k_ref[:, rows], qt_ref[rows, cols])
                expo = jnp.exp2(scores - jnp.max(scores, axis=0, keepdims=True)).astype(BF16)
                att_ref[rows, cols] = finish(dot(values, expo))
            return carry

        lax.fori_loop(0, length // 256, step, 0)


def row_kernel(
    edges, halo, center, inner, wconv, bias, gain, wq_t, wk, wv_t, wout, out_ref,
    taps, hidden, normed, k_ref, qt_ref, vt_ref, att_ref, first,
):
    index = pl.program_id(0)
    length = hidden.shape[0]
    above = 2 * index if edges else 0
    flat = (length, C)
    taps[0:8, :] = jnp.zeros((8, 3 * C), F32)
    taps[length + 8 : length + 16, :] = jnp.zeros((8, 3 * C), F32)
    part = 256
    per = part // center.shape[1]
    for start in range(0, length, part):
        src = slice(start // center.shape[1], start // center.shape[1] + per)
        total = dot(halo[src].reshape(part, C), wconv[above])
        total = total + dot(center[src].reshape(part, C), wconv[1])
        total = total + dot(inner[src].reshape(part, C), wconv[2 - above])
        taps[8 + start : 8 + start + part, :] = total
    for start in range(0, length, part):
        src = slice(start // center.shape[1], start // center.shape[1] + per)
        at = 8 + start
        pre = (
            taps[at - 1 : at - 1 + part, 0:C]
            + taps[at : at + part, C : 2 * C]
            + taps[at + 1 : at + 1 + part, 2 * C : 3 * C]
            + bias[...]
        )
        h = (center[src].reshape(part, C).astype(F32) + jax.nn.gelu(pre)).astype(BF16)
        hidden[start : start + part, :] = h
        normed[start : start + part, :] = normalize(h.astype(F32), gain[...])
    safe = projections(normed[...], wq_t[...], wk[...], wv_t[...], k_ref, qt_ref, vt_ref)
    attend(safe, k_ref, qt_ref, vt_ref, att_ref, length, 512)
    result = hidden[...].astype(F32) + dot_tn(att_ref[...], wout[...])

    @pl.when(index == 0)
    def _():
        first[...] = result

    @pl.when(index == 1)
    def _():
        pair = [first[...].reshape(length // 8, 8, C), result.reshape(length // 8, 8, C)]
        out_ref[...] = jnp.concatenate(pair, axis=1).astype(BF16)


def whole(shape):
    return pl.BlockSpec(shape, lambda i: (0,) * len(shape))


def row_call(edges, halo, rows, wconv, bias, gain, wq_t, wk, wv_t, wout):
    devices, _, cols, _ = rows.shape
    length = devices * cols
    block = (devices, None, cols, C)
    if edges:
        maps = (lambda i: (0, i, 0, 0), lambda i: (0, 3 * i, 0, 0), lambda i: (0, 1 + i, 0, 0))
    else:
        maps = (lambda i: (0, i, 0, 0), lambda i: (0, i + 1, 0, 0), lambda i: (0, i + 2, 0, 0))
    weights = [wconv, bias, gain, wq_t, wk, wv_t, wout]
    flops = 2 * length * C * (9 * C + 4 * C) * 2 + 2 * 2 * HEADS * length * length * 512
    return pl.pallas_call(
        functools.partial(row_kernel, edges),
        grid=(2,),
        in_specs=[pl.BlockSpec(block, m) for m in maps] + [whole(w.shape) for w in weights],
        out_specs=whole((length // 8, 16, C)),
        out_shape=jax.ShapeDtypeStruct((length // 8, 16, C), BF16),
        scratch_shapes=[
            pltpu.VMEM((length + 16, 3 * C), F32),
            pltpu.VMEM((length, C), BF16),
            pltpu.VMEM((length, C), BF16),
            pltpu.VMEM((length, C), BF16),
            pltpu.VMEM((C, length), BF16),
            pltpu.VMEM((C, length), BF16),
            pltpu.VMEM((C, length), BF16),
            pltpu.VMEM((length, C), F32),
        ],
        cost_estimate=pl.CostEstimate(
            flops=flops, bytes_accessed=8 * length * C, transcendentals=2 * HEADS * length**2
        ),
        compiler_params=pltpu.CompilerParams(vmem_limit_bytes=VMEM_LIMIT),
        name="edge_rows" if edges else "middle_rows",
    )(halo, rows, rows, *weights)


def col_kernel(
    middle, edge, gain, wq_t, wk, wv_t, wout, out_ref,
    left, right, k_ref, qt_ref, vt_ref, att_ref,
):
    index = pl.program_id(0)
    length = k_ref.shape[0]
    groups = length // 4

    @pl.when(index == 0)
    def _():
        mid = middle[...].astype(F32)
        out = edge[...].astype(F32)
        order = [out[:, :8], mid, out[:, 8:]]
        whole_cells = jnp.concatenate(order, axis=1).reshape(8 * length, C)
        left[...] = whole_cells[:, :128]
        right[...] = whole_cells[:, 128:]

    mine = pl.ds(index, length, stride=8)
    column = jnp.concatenate([left[mine, :], right[mine, :]], axis=1)
    normed = normalize(column, gain[...])
    safe = projections(normed, wq_t[...], wk[...], wv_t[...], k_ref, qt_ref, vt_ref)
    attend(safe, k_ref, qt_ref, vt_ref, att_ref, length, 512)
    result = column + dot_tn(att_ref[...], wout[...])
    left[mine, :] = result[:, :128]
    right[mine, :] = result[:, 128:]

    @pl.when(index == 7)
    def _():
        blocks = out_ref.shape[0]
        for half, ref in enumerate((left, right)):
            values = ref[...].reshape(groups // blocks, blocks, 32, 128)
            for block in range(blocks):
                part = values[:, block].reshape(length * 8 // blocks, 128)
                out_ref[block, :, 128 * half : 128 * half + 128] = part.astype(BF16)


def col_call(middle, edge, gain, wq_t, wk, wv_t, wout, blocks):
    length = middle.shape[0] * 4
    weights = [gain, wq_t, wk, wv_t, wout]
    shape = (blocks, length * 8 // blocks, C)
    flops = 8 * (2 * length * C * 4 * C + 2 * 2 * HEADS * length * length * 256)
    return pl.pallas_call(
        col_kernel,
        grid=(8,),
        in_specs=[whole(a.shape) for a in [middle, edge] + weights],
        out_specs=whole(shape),
        out_shape=jax.ShapeDtypeStruct(shape, BF16),
        scratch_shapes=[
            pltpu.VMEM((8 * length, 128), F32),
            pltpu.VMEM((8 * length, 128), F32),
            pltpu.VMEM((length, C), BF16),
            pltpu.VMEM((C, length), BF16),
            pltpu.VMEM((C, length), BF16),
            pltpu.VMEM((C, length), BF16),
        ],
        cost_estimate=pl.CostEstimate(
            flops=flops, bytes_accessed=32 * length * C, transcendentals=8 * HEADS * length**2
        ),
        compiler_params=pltpu.CompilerParams(vmem_limit_bytes=VMEM_LIMIT),
        name="columns",
    )(middle, edge, *weights)


def split_weights(qkv):
    return qkv[:, :C].T, qkv[:, C : 2 * C], qkv[:, 2 * C :].T


def shards(
    radar_input, conv_weight, conv_bias, row_gain, row_qkv, row_out, col_gain, col_qkv, col_out
):
    gy, gx = lax.axis_size("gy"), lax.axis_size("gx")
    height, cols, _ = radar_input.shape
    wconv = conv_weight.transpose(0, 2, 1, 3).reshape(3, C, 3 * C)
    row_weights = (wconv, conv_bias.reshape(1, C), row_gain.reshape(1, C)) + split_weights(row_qkv)
    col_weights = (col_gain.reshape(1, C),) + split_weights(col_qkv)
    rows = radar_input.reshape(gx, height // gx, cols, C)
    rows = lax.all_to_all(rows, "gx", split_axis=0, concat_axis=0, tiled=True)
    count = gy * gx
    up = [(i, i + 1) for i in range(count - 1)]
    down = [(j, i) for i, j in up]
    above = lax.ppermute(rows[:, 3], ("gy", "gx"), up)
    below = lax.ppermute(rows[:, 0], ("gy", "gx"), down)
    middle = row_call(False, rows, rows, *row_weights, row_out)
    halo = jnp.stack([above, below], axis=1)
    edge = row_call(True, halo, rows, *row_weights, row_out)
    middle = lax.all_to_all(middle, ("gx", "gy"), split_axis=0, concat_axis=0, tiled=True)
    edge = lax.all_to_all(edge, ("gx", "gy"), split_axis=0, concat_axis=0, tiled=True)
    result = col_call(middle, edge, *col_weights, col_out, gy)
    result = lax.all_to_all(result, "gy", split_axis=0, concat_axis=0, tiled=True)
    result = result.reshape(gy, height, cols // gy, C).transpose(1, 0, 2, 3)
    return result.reshape(height, cols, C)


def solution(mesh):
    in_specs = (P("gy", "gx", None), P(), P(), P(), P(), P(), P(), P(), P())
    out_specs = P("gy", "gx", None)
    return jax.shard_map(shards, mesh=mesh, in_specs=in_specs, out_specs=out_specs, check_vma=False)
```

time: 598 us -> 290 us (0.48); the launches traced: 587 us -> 289 us
  matrix products: 223 us -> 0 us
  Pallas kernels: 0 us -> 171 us
  blocking collectives: 136 us -> 30.1 us
  local copies, waits for them, and re-layouts: 93.3 us -> 12.2 us
  waiting for transfers between devices: 84.9 us -> 40.8 us
  other arithmetic: 22.6 us -> 1.14 us
  starting transfers between devices: 27.1 us -> 34 us
    pallas_call x0 -> x3, Pallas kernels: none -> 171 us  [the longest x2 107 us: row_call(): pl.pallas_call(functools.partial(row_kernel, edges), grid=(2,), in_specs=...]
    dot_general x29 -> x0, matrix products: 115 us -> none  [the longest x16 101 us: sequence_attention(): jnp.einsum('hqk,khd->qhd', weights, vh, preferred_element_type=jnp.float32)]
    sub x16 -> x0, matrix products: 108 us -> none  [sequence_attention(): expo = jnp.exp(scores - top)]
    all_to_all x4 -> x1, blocking collectives: 136 us -> 30.1 us  [shards(): lax.all_to_all(result, 'gy', split_axis=0, concat_axis=0, tiled=True)]
    all_to_all x4 -> x3, waiting for transfers between devices: 76.8 us -> 40.8 us  [the longest x1 23.9 us: shards(): rows = lax.all_to_all(rows, 'gx', split_axis=0, concat_axis=0, tiled=True)]
    dynamic_slice x28 -> x0, local copies, waits for them, and re-layouts: 23 us -> none  [the longest x16 14.5 us: step(): one_k = lax.dynamic_index_in_dim(keys, index, axis, keepdims=False)]
    while x13 -> x0, local copies, waits for them, and re-layouts: 21.7 us -> none  [the longest x5 20.5 us: attend_all(): return lax.fori_loop(0, count, step, jnp.zeros(queries.shape, jnp.bfloat16))]
    all_to_all x8 -> x0, local copies, waits for them, and re-layouts: 19.3 us -> none  [the longest x1 4.18 us: shards(): lax.all_to_all(values, 'gy', split_axis=1, concat_axis=0, tiled=True)]
  transfers between devices with their start and end apart: 8 -> 5, of which waited for: 7 -> 2; matrix products, arithmetic and copies ran while one was open for 5% -> 3% of each run, Pallas kernels for 0% -> 37%
where the time goes in v1:
time: 290 us; the launch traced here: 289 us
  Pallas kernels  171 us (59%)
  waiting for transfers between devices  40.8 us (14%)
  starting transfers between devices  34 us (12%)
  blocking collectives  30.1 us (10%)
  local copies, waits for them, and re-layouts  12.2 us (4%)
    pallas_call x2, Pallas kernels, row_call(): pl.pallas_call(functools.partial(row_kernel, edges), grid=(2,), in_specs=...  107 us
    pallas_call x1, Pallas kernels, col_call(): pl.pallas_call(col_kernel, grid=(8,), in_specs=[whole(a.shape) for a in [...  63.7 us
    all_to_all x1, blocking collectives, shards(): lax.all_to_all(result, 'gy', split_axis=0, concat_axis=0, tiled=True)  30.1 us
    all_to_all x1, waiting for transfers between devices, shards(): rows = lax.all_to_all(rows, 'gx', split_axis=0, concat_axis=0, tiled=True)  23.9 us
    all_to_all x1, waiting for transfers between devices, shards(): lax.all_to_all(edge, ('gx', 'gy'), split_axis=0, concat_axis=0, tiled=True)  17 us
    all_to_all x1, starting transfers between devices, shards(): lax.all_to_all(middle, ('gx', 'gy'), split_axis=0, concat_axis=0, tiled=T...  11.7 us
    all_to_all x1, starting transfers between devices, shards(): lax.all_to_all(edge, ('gx', 'gy'), split_axis=0, concat_axis=0, tiled=True)  9.99 us
    all_to_all x1, starting transfers between devices, shards(): rows = lax.all_to_all(rows, 'gx', split_axis=0, concat_axis=0, tiled=True)  7.25 us
  transfers between devices with their start and end apart: 5, of which 2 were waited for; matrix products, arithmetic and copies ran while one was open for 3% of the time, Pallas kernels for 37%

profile of v1, /device:TPU:0, one launch (start us, length us, event | category | flops | bytes accessed | tf_op | source)
XLA Modules:
  0.0 289.2 jit_solution(6980109053053833883)
XLA Ops:
  0.0 0.0 copy-start.3
  0.0 7.2 %all-to-all-start = ((bf16[16,4,64,256]{3,2,1,0:T(8,128)(2,1)}), bf16[16,4,64,256]{3,2,1,0:T(8,128)(2,1)S(1)}, u32[]{:S(2)}, u32[]{:S(2)}) async-start(bf16[16,4,64,256]{3,2,1,0:T(8,128)(2,1)} %bitcast.27), calls=%async_computation | async-start | bytes 4194304 | tf_op jit(solution)/shard_map/all_to_all | solution.py:250
  7.3 0.0 copy-done.3
  7.3 0.7 fusion.1
  8.0 0.8 copy.28
  8.7 0.8 copy.29
  9.5 1.6 copy.18
  11.0 1.6 copy.21.wconv
  12.6 23.9 %all-to-all-done.halo.center.inner = bf16[16,4,64,256]{3,2,1,0:T(8,128)(2,1)S(1)} async-done(((bf16[16,4,64,256]{3,2,1,0:T(8,128)(2,1)}), bf16[16,4,64,256]{3,2,1,0:T(8,128)(2,1)S(1)}, u32[]{:S(2)}, u32[]{:S(2)}) %all-to-all-start) | async-done | bytes 2097184 | tf_op jit(solution)/shard_map/all_to_all | solution.py:250
  36.5 0.0 copy-start
  36.5 1.0 slice_bitcast_fusion.1
  37.5 1.3 collective-permute-start.1
  38.8 3.8 %collective-permute-start = (bf16[16,64,256]{2,1,0:T(8,128)(2,1)S(1)}, bf16[16,64,256]{2,1,0:T(8,128)(2,1)}, u32[]{:S(2)}, u32[]{:S(2)}) collective-permute-start(bf16[16,64,256]{2,1,0:T(8,128)(2,1)S(1)} %get-tuple-element.5), channel_id=1, source_target_pairs={{0,1},{1,2},{2,3},{3,4},{4,5},{5,6},{6,7},{7,8},{8,9},{9,10},{10,1... | collective-permute-start | bytes 1572872 | tf_op jit(solution)/shard_map/ppermute | solution.py:254
  42.6 0.0 copy-done
  42.6 53.5 %middle_rows.1 = bf16[128,16,256]{2,1,0:T(8,128)(2,1)} custom-call(bf16[16,4,64,256]{3,2,1,0:T(8,128)(2,1)} %copy-done, bf16[16,4,64,256]{3,2,1,0:T(8,128)(2,1)} %copy-done, bf16[16,4,64,256]{3,2,1,0:T(8,128)(2,1)} %copy-done, bf16[3,256,768]{2,1,0:T(8,128)(2,1)} %copy.21.wconv, f32[1,256]{1,0:T(1,128)} %bitcast.35, f32[1,256]{1,0:T(1,128)} %bitcast.37, ...), custom_call_target="tpu_custom_call" | custom-call | flops 20669530112 | bytes 2097152 | tf_op jit(solution)/shard_map/middle_rows/pallas_call | solution.py:150
  96.1 11.7 %all-to-all-start.1 = ((bf16[128,16,256]{2,1,0:T(8,128)(2,1)}), bf16[128,16,256]{2,1,0:T(8,128)(2,1)S(1)}, u32[]{:S(2)}, u32[]{:S(2)}) async-start(bf16[128,16,256]{2,1,0:T(8,128)(2,1)} %middle_rows.1), calls=%async_computation.1 | async-start | bytes 2097152 | tf_op jit(solution)/shard_map/all_to_all | solution.py:259
  107.8 0.0 collective-permute-done.1
  107.8 0.0 collective-permute-done
  107.9 1.1 pad_maximum_fusion
  109.0 1.0 copy.23.halo
  110.0 53.5 %edge_rows.1 = bf16[128,16,256]{2,1,0:T(8,128)(2,1)} custom-call(bf16[16,2,64,256]{3,2,1,0:T(8,128)(2,1)} %copy.23.halo, bf16[16,4,64,256]{3,2,1,0:T(8,128)(2,1)} %copy-done, bf16[16,4,64,256]{3,2,1,0:T(8,128)(2,1)} %copy-done, bf16[3,256,768]{2,1,0:T(8,128)(2,1)} %copy.21.wconv, f32[1,256]{1,0:T(1,128)} %bitcast.36, f32[1,256]{1,0:T(1,128)} %bitcast.38, ...), custom_call_target="tpu_custom_call" | custom-call | flops 20669530112 | bytes 2097152 | tf_op jit(solution)/shard_map/edge_rows/pallas_call | solution.py:150
  163.5 0.0 copy-start.4
  163.5 0.0 all-to-all-done.1.middle
  163.6 0.0 copy-start.1
  163.6 10.0 %all-to-all-start.2 = ((bf16[128,16,256]{2,1,0:T(8,128)(2,1)}), bf16[128,16,256]{2,1,0:T(8,128)(2,1)S(1)}, u32[]{:S(2)}, u32[]{:S(2)}) async-start(bf16[128,16,256]{2,1,0:T(8,128)(2,1)} %edge_rows.1), calls=%async_computation.2 | async-start | bytes 2097152 | tf_op jit(solution)/shard_map/all_to_all | solution.py:260
  173.6 0.0 copy-done.4
  173.6 0.7 fusion
  174.2 0.7 copy.31
  175.0 0.8 copy.32
  175.7 17.0 %all-to-all-done.2.edge = bf16[128,16,256]{2,1,0:T(8,128)(2,1)S(1)} async-done(((bf16[128,16,256]{2,1,0:T(8,128)(2,1)}), bf16[128,16,256]{2,1,0:T(8,128)(2,1)S(1)}, u32[]{:S(2)}, u32[]{:S(2)}) %all-to-all-start.2) | async-done | bytes 1048608 | tf_op jit(solution)/shard_map/all_to_all | solution.py:260
  192.7 0.0 copy-start.2
  192.7 0.0 copy-done.1
  192.7 1.0 copy-done.2
  193.7 63.7 %columns.1 = bf16[8,512,256]{2,1,0:T(8,128)(2,1)} custom-call(bf16[128,16,256]{2,1,0:T(8,128)(2,1)} %copy-done.1, bf16[128,16,256]{2,1,0:T(8,128)(2,1)} %copy-done.2, f32[1,256]{1,0:T(1,128)} %bitcast.39, bf16[256,256]{1,0:T(8,128)(2,1)} %bitcast.33, bf16[256,256]{1,0:T(8,128)(2,1)} %get-tuple-element.9.wk, bf16[256,256]{1,0:T(8,128)(2,1)} %bitcast.34, ...), custom_call_target="tpu_custom_call" | custom-call | flops 19327352832 | bytes 4194304 | tf_op jit(solution)/shard_map/columns/pallas_call | solution.py:215
  257.4 30.1 %all_to_all.20 = bf16[8,512,256]{2,1,0:T(8,128)(2,1)S(1)} all-to-all(bf16[8,512,256]{2,1,0:T(8,128)(2,1)} %columns.1), channel_id=1, replica_groups=mesh['gy'=8,'gx'=16] {'gy'}, dimensions={0} | all-to-all | bytes 4194304 | tf_op jit(solution)/shard_map/all_to_all | solution.py:262
  287.6 1.6 copy_bitcast_fusion
Async XLA Ops:
  0.0 7.3 %copy-start.3 = (bf16[256,768]{1,0:T(8,128)(2,1)S(1)}, bf16[256,768]{1,0:T(8,128)(2,1)}, u32[]{:S(2)}) copy-start(bf16[256,768]{1,0:T(8,128)(2,1)} %param.13) | copy-start | bytes 1179652
  0.0 36.5 %all-to-all-start = ((bf16[16,4,64,256]{3,2,1,0:T(8,128)(2,1)}), bf16[16,4,64,256]{3,2,1,0:T(8,128)(2,1)S(1)}, u32[]{:S(2)}, u32[]{:S(2)}) async-start(bf16[16,4,64,256]{3,2,1,0:T(8,128)(2,1)} %bitcast.27), calls=%async_computation | async-start | bytes 4194304 | tf_op jit(solution)/shard_map/all_to_all | solution.py:250
  36.5 6.1 %copy-start = (bf16[16,4,64,256]{3,2,1,0:T(8,128)(2,1)}, bf16[16,4,64,256]{3,2,1,0:T(8,128)(2,1)S(1)}, u32[]{:S(2)}) copy-start(bf16[16,4,64,256]{3,2,1,0:T(8,128)(2,1)S(1)} %all-to-all-done.halo.center.inner) | copy-start | bytes 6291460
  37.5 70.3 %collective-permute-start.1 = (bf16[16,64,256]{2,1,0:T(8,128)(2,1)}, bf16[16,64,256]{2,1,0:T(8,128)(2,1)S(1)}, u32[]{:S(2)}, u32[]{:S(2)}) collective-permute-start(bf16[16,64,256]{2,1,0:T(8,128)(2,1)} %get-tuple-element.6), channel_id=1, source_target_pairs={{1,0},{2,1},{3,2},{4,3},{5,4},{6,5},{7,6},{8,7},{9,8},{10,9},{11,1... | collective-permute-start | bytes 1572872 | tf_op jit(solution)/shard_map/ppermute | solution.py:255
  38.8 69.1 %collective-permute-start = (bf16[16,64,256]{2,1,0:T(8,128)(2,1)S(1)}, bf16[16,64,256]{2,1,0:T(8,128)(2,1)}, u32[]{:S(2)}, u32[]{:S(2)}) collective-permute-start(bf16[16,64,256]{2,1,0:T(8,128)(2,1)S(1)} %get-tuple-element.5), channel_id=1, source_target_pairs={{0,1},{1,2},{2,3},{3,4},{4,5},{5,6},{6,7},{7,8},{8,9},{9,10},{10,1... | collective-permute-start | bytes 1572872 | tf_op jit(solution)/shard_map/ppermute | solution.py:254
  96.1 67.4 %all-to-all-start.1 = ((bf16[128,16,256]{2,1,0:T(8,128)(2,1)}), bf16[128,16,256]{2,1,0:T(8,128)(2,1)S(1)}, u32[]{:S(2)}, u32[]{:S(2)}) async-start(bf16[128,16,256]{2,1,0:T(8,128)(2,1)} %middle_rows.1), calls=%async_computation.1 | async-start | bytes 2097152 | tf_op jit(solution)/shard_map/all_to_all | solution.py:259
  163.5 10.0 %copy-start.4 = (bf16[256,768]{1,0:T(8,128)(2,1)S(1)}, bf16[256,768]{1,0:T(8,128)(2,1)}, u32[]{:S(2)}) copy-start(bf16[256,768]{1,0:T(8,128)(2,1)} %param.16) | copy-start | bytes 1179652
  163.6 29.2 %copy-start.1 = (bf16[128,16,256]{2,1,0:T(8,128)(2,1)}, bf16[128,16,256]{2,1,0:T(8,128)(2,1)S(1)}, u32[]{:S(2)}) copy-start(bf16[128,16,256]{2,1,0:T(8,128)(2,1)S(1)} %all-to-all-done.1.middle) | copy-start | bytes 3145732
  163.6 29.2 %all-to-all-start.2 = ((bf16[128,16,256]{2,1,0:T(8,128)(2,1)}), bf16[128,16,256]{2,1,0:T(8,128)(2,1)S(1)}, u32[]{:S(2)}, u32[]{:S(2)}) async-start(bf16[128,16,256]{2,1,0:T(8,128)(2,1)} %edge_rows.1), calls=%async_computation.2 | async-start | bytes 2097152 | tf_op jit(solution)/shard_map/all_to_all | solution.py:260
  192.7 1.0 copy-start.2
